TPU v7x, 32 devices: a whole 2x2x4 slice. The times are simulated.
32 devices in a mesh: dp: 8 (over y, x, core), tensor: 4 (over z).
Axes of the slice: x: 2, y: 2, z: 4, core: 2. Of those that a mesh axis runs over, the one named last changes fastest.
Arguments:
- gradient: float32 [96, 512, 512], P('dp', 'tensor'), may hold values from -150 to 150
- second_moment: float32 [96, 512, 512], P('dp', 'tensor'), may hold values from 0.5 to 4
- momentum: float32 [96, 512, 512], P('dp', 'tensor'), may hold values from -6 to 6
- left_state: float32 [8, 16, 512, 512], P('dp', 'tensor'), as said below
- right_state: float32 [8, 16, 512, 512], P('dp', 'tensor'), as said below
- owner: int32 [96, 1], P('dp'), may hold values from 0 to 7; in each aligned block of 12 rows (0 to 11, 12 to 23, ...) at most 2 rows name the same one
Outputs:
- direction: float32 [96, 512, 512], P('dp', 'tensor')
- moment_new: float32 [96, 512, 512], P('dp', 'tensor')
- left_new: float32 [8, 16, 512, 512], P('dp', 'tensor')
- right_new: float32 [8, 16, 512, 512], P('dp', 'tensor')
Inputs may be any that keep to these rules, and one draw needn't show every extreme that they name: Among the 12 blocks of one dp index at most 2 name the same owner, and in every draw some dp index gives exactly 2 blocks to one owner. `left_state`: each slot's matrix is symmetric positive definite. `right_state`: each slot's matrix is symmetric positive definite.
All inputs are finite; a program needn't handle non-finite values.
Results may differ from a plain program's by a relative error of at most 0.0001.
Values sent between devices are 32-bit elements; how exact they have to be, the bound alone decides.
A program may use at most 128 MiB of HBM per device.

v0:
```python
import jax
import jax.numpy as jnp
from jax import lax
from jax.sharding import PartitionSpec as P

BLOCK = 512
PAIR_MOST = 2
NEWTON = 2


factor_decay = 0.9
root_eps = 0.001
adam_decay = 0.999
adam_eps = 1e-08
momentum_decay = 0.9
mean_eps = 1e-06


def product(left, right):
    return jnp.dot(left, right, precision=lax.Precision.HIGHEST)


def inverse_root(matrix):
    eye = jnp.eye(matrix.shape[0], dtype=jnp.float32)
    shifted = matrix + root_eps * eye
    scale = jnp.sqrt(jnp.sum(shifted * shifted))
    iterate = shifted / scale
    coefficient = scale ** (-0.25)
    result = eye
    for turn in range(NEWTON):
        factor = (5.0 * eye - iterate) * 0.25
        if turn == 0:
            result = coefficient * factor
        else:
            result = product(result, factor)
        if turn + 1 < NEWTON:
            square = product(factor, factor)
            fourth = product(square, square)
            iterate = product(fourth, iterate)
    return result


def precondition(block, left_old, right_old):
    left_next = factor_decay * left_old + (1.0 - factor_decay) * product(block, block.T)
    right_next = factor_decay * right_old + (1.0 - factor_decay) * product(block.T, block)
    left_root = inverse_root(left_next)
    right_root = inverse_root(right_next)
    result = product(product(left_root, block), right_root)
    return (left_next, right_next, result)


def per_device(gradient, second_moment, momentum, left_state, right_state, owner):
    dp_count = lax.axis_size("dp")
    tensor_count = lax.axis_size("tensor")
    blocks_here = gradient.shape[0]
    slots_dp = PAIR_MOST * dp_count
    owners = owner[:, 0]
    position = jnp.arange(blocks_here, dtype=jnp.int32)
    earlier = (owners[:, None] == owners[None, :]) & (position[None, :] < position[:, None])
    rank = jnp.sum(earlier.astype(jnp.int32), axis=1)
    target = owners * PAIR_MOST + rank
    select = (target[None, :] == jnp.arange(slots_dp, dtype=jnp.int32)[:, None]).astype(jnp.float32)
    outgoing = jnp.einsum("sk,krc->src", select, gradient, precision=lax.Precision.HIGHEST)
    marks = jnp.broadcast_to(jnp.sum(select, axis=1, keepdims=True), (slots_dp, tensor_count))
    moment_new = adam_decay * second_moment + (1.0 - adam_decay) * gradient * gradient
    adam = gradient / (jnp.sqrt(moment_new) + adam_eps)
    adam_part = jnp.sum(adam * adam, axis=(1, 2))
    arrived, arrived_marks = (
        lax.all_to_all(
            lax.all_to_all(outgoing, "dp", split_axis=0, concat_axis=0, tiled=True),
            "tensor",
            split_axis=0,
            concat_axis=1,
            tiled=True,
        ),
        lax.all_to_all(
            lax.all_to_all(marks, "dp", split_axis=0, concat_axis=0, tiled=True),
            "tensor",
            split_axis=0,
            concat_axis=1,
            tiled=True,
        ),
    )
    left_old = left_state[0]
    right_old = right_state[0]
    lefts = []
    rights = []
    results = []
    for slot_index in range(arrived.shape[0]):
        block = arrived[slot_index]
        left_slot = left_old[slot_index]
        right_slot = right_old[slot_index]
        left_next, right_next, result = precondition(block, left_slot, right_slot)
        lefts.append(left_next)
        rights.append(right_next)
        results.append(result)
    left_new = jnp.stack(lefts)[None]
    right_new = jnp.stack(rights)[None]
    precond = jnp.stack(results)
    homeward = (precond,)
    by_blocks = (
        lax.all_to_all(
            lax.all_to_all(homeward[0], "tensor", split_axis=1, concat_axis=0, tiled=True),
            "dp",
            split_axis=0,
            concat_axis=0,
            tiled=True,
        ),
    )
    returned = jnp.einsum("sk,src->krc", select, by_blocks[0], precision=lax.Precision.HIGHEST)
    pre_part = jnp.sum(returned * returned, axis=(1, 2))
    adam_sum, pre_sum = lax.psum((adam_part, pre_part), "tensor")
    area = float(BLOCK * BLOCK)
    ratio = jnp.sqrt(adam_sum / area / (pre_sum / area + mean_eps))
    direction = momentum_decay * momentum + ratio[:, None, None] * returned
    return (direction, moment_new, left_new, right_new)


def solution(mesh):
    return jax.shard_map(
        per_device,
        mesh=mesh,
        in_specs=(
            P("dp", "tensor", None),
            P("dp", "tensor", None),
            P("dp", "tensor", None),
            P("dp", "tensor", None, None),
            P("dp", "tensor", None, None),
            P("dp", None),
        ),
        out_specs=(
            P("dp", "tensor", None),
            P("dp", "tensor", None),
            P("dp", "tensor", None, None),
            P("dp", "tensor", None, None),
        ),
        check_vma=False,
    )
```

profile of v0, /device:TPU:0, one launch (start us, length us, event | category | flops | bytes accessed | tf_op | source)
XLA Modules:
  0.0 480.9 jit_solution(17687856220403210205)
XLA Ops:
  2.2 5.7 %fusion.2 = f32[16,128,512]{2,0,1:T(8,128)S(1)} fusion(f32[12,128,512]{2,1,0:T(8,128)} %param.6, s32[12]{0:T(128)S(1)} %multiply_add_fusion), kind=kOutput, calls=%fused_computation.23 | convolution fusion | flops 150995136 | bytes 7340080 | tf_op jit(solution)/shard_map/sk,krc->src/dot_general | solution.py:63
  10.3 54.0 %all_to_all.43 = f32[16,128,512]{2,1,0:T(8,128)S(1)} all-to-all(f32[16,128,512]{2,1,0:T(8,128)S(1)} %copy.48), channel_id=1, replica_groups=mesh['dp'=8,'tensor'=4] {'dp'}, dimensions={0} | all-to-all | bytes 8388608 | tf_op jit(solution)/shard_map/all_to_all | solution.py:70
  64.3 97.3 %all_to_all.44 = f32[16,128,512]{2,1,0:T(8,128)S(1)} all-to-all(f32[16,128,512]{2,1,0:T(8,128)S(1)} %all_to_all.43), channel_id=1, replica_groups=mesh['dp'=8,'tensor'=4] {'tensor'}, dimensions={0} | all-to-all | bytes 8388608 | tf_op jit(solution)/shard_map/all_to_all | solution.py:69
  167.4 3.6 multiply_reduce_fusion.8
  171.0 3.5 multiply_reduce_fusion.6
  180.3 3.7 fusion.30
  189.7 3.8 fusion.54
  199.0 3.7 fusion.46
  208.6 3.7 fusion.38
  217.1 4.7 multiply_reduce_fusion.3
  222.5 3.8 fusion.34
  235.0 4.7 multiply_reduce_fusion.9
  240.4 3.7 fusion.58
  253.0 3.9 multiply_reduce_fusion.5
  267.7 3.9 multiply_reduce_fusion.7
  301.2 95.2 %all_to_all.45 = f32[4,512,512]{2,0,1:T(4,128)S(1)} all-to-all(f32[4,512,512]{2,0,1:T(4,128)S(1)} %copy.54), channel_id=1, replica_groups=mesh['dp'=8,'tensor'=4] {'tensor'}, dimensions={1} | all-to-all | bytes 8388608 | tf_op jit(solution)/shard_map/all_to_all | solution.py:103
  399.7 5.1 %all-to-all-start.3 = ((f32[16,128,512]{2,1,0:T(8,128)}), f32[16,128,512]{2,1,0:T(8,128)}, u32[]{:S(2)}, u32[]{:S(2)}) async-start(f32[16,128,512]{2,1,0:T(8,128)} %bitcast.157), calls=%async_computation.3 | async-start | bytes 8388608 | tf_op jit(solution)/shard_map/all_to_all | solution.py:102
  404.8 5.3 %multiply_reduce_fusion.1 = (f32[12]{0:T(128)S(1)}, f32[12,128,512]{2,1,0:T(8,128)}) fusion(f32[12,128,512]{2,1,0:T(8,128)S(1)} %copy-done, f32[12,128,512]{2,1,0:T(8,128)} %param.7), kind=kLoop, calls=%fused_computation.37 | loop fusion | flops 6291444 | bytes 9437232 | tf_op jit(solution)/shard_map/reduce_sum | solution.py:67
  410.2 3.8 maximum_bitcast_fusion
  414.1 39.8 %all-to-all-done.3 = f32[16,128,512]{2,1,0:T(8,128)} async-done(((f32[16,128,512]{2,1,0:T(8,128)}), f32[16,128,512]{2,1,0:T(8,128)}, u32[]{:S(2)}, u32[]{:S(2)}) %all-to-all-start.3) | async-done | bytes 4194336 | tf_op jit(solution)/shard_map/all_to_all | solution.py:102
  453.9 8.9 %multiply_reduce_fusion = (f32[12]{0:T(128)S(1)}, f32[12,128,512]{2,0,1:T(8,128)}) fusion(f32[16,128,512]{2,1,0:T(8,128)} %all-to-all-done.3, s32[12]{0:T(128)S(1)} %multiply_add_fusion), kind=kOutput, calls=%fused_computation.27 | convolution fusion | flops 152567984 | bytes 7340128 | tf_op jit(solution)/shard_map/sk,src->krc/dot_general | solution.py:110
  462.8 9.6 %all-reduce = (f32[12]{0:T(128)S(1)}, f32[12]{0:T(128)S(1)}) all-reduce(f32[12]{0:T(128)S(1)} %get-tuple-element.44, f32[12]{0:T(128)S(1)} %get-tuple-element.22), channel_id=1, replica_groups=mesh['dp'=8,'tensor'=4] {'tensor'}, use_global_device_ids=true, to_apply=%region_12.0 | all-reduce | flops 24 | bytes 192 | tf_op jit(solution)/shard_map/psum | solution.py:112
  472.4 4.5 fusion.4
  476.9 3.5 copy.57
  (107 shorter events, 93.7 us)
Async XLA Ops:
  180.3 5.8 %copy-start.14 = (f32[512,512]{1,0:T(8,128)S(1)}, f32[512,512]{1,0:T(8,128)}, u32[]{:S(2)}) copy-start(f32[512,512]{1,0:T(8,128)} %get-tuple-element.31) | copy-start | bytes 3145732
  189.7 5.6 %copy-start.17 = (f32[512,512]{1,0:T(8,128)S(1)}, f32[512,512]{1,0:T(8,128)}, u32[]{:S(2)}) copy-start(f32[512,512]{1,0:T(8,128)} %get-tuple-element.43) | copy-start | bytes 3145732
  199.0 5.6 %copy-start.20 = (f32[512,512]{1,0:T(8,128)S(1)}, f32[512,512]{1,0:T(8,128)}, u32[]{:S(2)}) copy-start(f32[512,512]{1,0:T(8,128)} %get-tuple-element.39) | copy-start | bytes 3145732
  208.6 5.6 %copy-start.23 = (f32[512,512]{1,0:T(8,128)S(1)}, f32[512,512]{1,0:T(8,128)}, u32[]{:S(2)}) copy-start(f32[512,512]{1,0:T(8,128)} %get-tuple-element.35) | copy-start | bytes 3145732
  212.3 4.8 copy-start.1
  222.5 5.6 %copy-start.3 = (f32[512,512]{1,0:T(8,128)S(1)}, f32[512,512]{1,0:T(8,128)}, u32[]{:S(2)}) copy-start(f32[512,512]{1,0:T(8,128)} %get-tuple-element.29) | copy-start | bytes 3145732
  240.4 5.6 %copy-start.5 = (f32[512,512]{1,0:T(8,128)S(1)}, f32[512,512]{1,0:T(8,128)}, u32[]{:S(2)}) copy-start(f32[512,512]{1,0:T(8,128)} %get-tuple-element.41) | copy-start | bytes 3145732
  256.9 6.5 %copy-start.7 = (f32[512,512]{1,0:T(8,128)}, f32[512,512]{1,0:T(8,128)S(1)}, u32[]{:S(2)}) copy-start(f32[512,512]{1,0:T(8,128)S(1)} %get-tuple-element.33) | copy-start | bytes 3145732
  271.7 6.5 %copy-start.10 = (f32[512,512]{1,0:T(8,128)}, f32[512,512]{1,0:T(8,128)S(1)}, u32[]{:S(2)}) copy-start(f32[512,512]{1,0:T(8,128)S(1)} %get-tuple-element.37) | copy-start | bytes 3145732
  278.2 4.1 copy-start.15
  278.2 4.1 copy-start.27
  280.2 4.1 copy-start.18
  280.2 4.1 copy-start.28
  399.7 5.1 %copy-start = (f32[12,128,512]{2,1,0:T(8,128)S(1)}, f32[12,128,512]{2,1,0:T(8,128)}, u32[]{:S(2)}) copy-start(f32[12,128,512]{2,1,0:T(8,128)} %param.6) | copy-start | bytes 9437188
  399.7 54.2 %all-to-all-start.3 = ((f32[16,128,512]{2,1,0:T(8,128)}), f32[16,128,512]{2,1,0:T(8,128)}, u32[]{:S(2)}, u32[]{:S(2)}) async-start(f32[16,128,512]{2,1,0:T(8,128)} %bitcast.157), calls=%async_computation.3 | async-start | bytes 8388608 | tf_op jit(solution)/shard_map/all_to_all | solution.py:102
  404.7 5.4 %copy-start.4 = (f32[512,512]{1,0:T(8,128)S(1)}, f32[512,512]{1,0:T(8,128)}, u32[]{:S(2)}) copy-start(f32[512,512]{1,0:T(8,128)} %get-tuple-element.29) | copy-start | bytes 3145732
  404.8 5.4 %copy-start.6 = (f32[512,512]{1,0:T(8,128)S(1)}, f32[512,512]{1,0:T(8,128)}, u32[]{:S(2)}) copy-start(f32[512,512]{1,0:T(8,128)} %get-tuple-element.41) | copy-start | bytes 3145732
  404.8 5.4 %copy-start.8 = (f32[512,512]{1,0:T(8,128)S(1)}, f32[512,512]{1,0:T(8,128)}, u32[]{:S(2)}) copy-start(f32[512,512]{1,0:T(8,128)} %copy-done.7) | copy-start | bytes 3145732
  404.8 5.4 %copy-start.11 = (f32[512,512]{1,0:T(8,128)S(1)}, f32[512,512]{1,0:T(8,128)}, u32[]{:S(2)}) copy-start(f32[512,512]{1,0:T(8,128)} %copy-done.10) | copy-start | bytes 3145732
  404.8 5.4 %copy-start.16 = (f32[512,512]{1,0:T(8,128)S(1)}, f32[512,512]{1,0:T(8,128)}, u32[]{:S(2)}) copy-start(f32[512,512]{1,0:T(8,128)} %get-tuple-element.31) | copy-start | bytes 3145732
  404.8 5.4 %copy-start.19 = (f32[512,512]{1,0:T(8,128)S(1)}, f32[512,512]{1,0:T(8,128)}, u32[]{:S(2)}) copy-start(f32[512,512]{1,0:T(8,128)} %get-tuple-element.43) | copy-start | bytes 3145732
  404.8 5.4 %copy-start.22 = (f32[512,512]{1,0:T(8,128)S(1)}, f32[512,512]{1,0:T(8,128)}, u32[]{:S(2)}) copy-start(f32[512,512]{1,0:T(8,128)} %get-tuple-element.39) | copy-start | bytes 3145732
  404.8 5.4 %copy-start.25 = (f32[512,512]{1,0:T(8,128)S(1)}, f32[512,512]{1,0:T(8,128)}, u32[]{:S(2)}) copy-start(f32[512,512]{1,0:T(8,128)} %get-tuple-element.35) | copy-start | bytes 3145732
  414.1 58.3 %copy-start.13 = (f32[12,128,512]{2,1,0:T(8,128)S(1)}, f32[12,128,512]{2,1,0:T(8,128)}, u32[]{:S(2)}) copy-start(f32[12,128,512]{2,1,0:T(8,128)} %param.8) | copy-start | bytes 9437188
  (8 other events, 18.1 us)
where the time goes:
time: 487 us; the launch traced here: 481 us
  blocking collectives  256 us (53%)
  matrix products  141 us (29%)
  waiting for transfers between devices  39.8 us (8%)
  local copies, waits for them, and re-layouts  15.8 us (3%)
  other arithmetic  15.7 us (3%)
  between operations  7.61 us (2%)
  starting transfers between devices  5.06 us (1%)
    dot_general x48, matrix products, product(): return jnp.dot(left, right, precision=lax.Precision.HIGHEST)  126 us
    all_to_all x1, blocking collectives, per_device(): lax.all_to_all(lax.all_to_all(outgoing, 'dp', split_axis=0, concat_axis=0...  97.3 us
    all_to_all x1, blocking collectives, per_device(): lax.all_to_all(homeward[0], 'tensor', split_axis=1, concat_axis=0, tiled=...  95.2 us
    all_to_all x1, blocking collectives, per_device(): lax.all_to_all(outgoing, 'dp', split_axis=0, concat_axis=0, tiled=True)  54 us
    all_to_all x1, waiting for transfers between devices, per_device(): lax.all_to_all(lax.all_to_all(homeward[0], 'tensor', split_axis=1, concat...  39.8 us
  transfers between devices with their start and end apart: 1, of which 1 were waited for; matrix products, arithmetic and copies ran while one was open for 2% of the time, Pallas kernels for 0%

commit v1 on v0

v1 whole, which is shorter than its diff:
```python
import functools

import jax
import jax.numpy as jnp
from jax import lax
from jax.experimental import pallas as pl
from jax.experimental.pallas import tpu as pltpu
from jax.sharding import PartitionSpec as P

PAIR_MOST = 2

factor_decay = 0.9
root_eps = 0.001
adam_decay = 0.999
adam_eps = 1e-08
momentum_decay = 0.9
mean_eps = 1e-06

MESH = pl.DeviceIdType.MESH
ROWS = 256

FOURTH = (2.44140625, -1.953125, 0.5859375, -0.078125, 0.00390625)
ROOT = (
    25.0 / 16.0,
    (-5.0 - 5.0 * FOURTH[0]) / 16.0,
    (-5.0 * FOURTH[1] + FOURTH[0]) / 16.0,
    (-5.0 * FOURTH[2] + FOURTH[1]) / 16.0,
    (-5.0 * FOURTH[3] + FOURTH[2]) / 16.0,
    (-5.0 * FOURTH[4] + FOURTH[3]) / 16.0,
    FOURTH[4] / 16.0,
)


def gather_kernel(source_ref, used_ref, gradient_ref, out_ref):
    used = used_ref[pl.program_id(0)] > 0
    out_ref[...] = jnp.where(used, gradient_ref[...], 0.0)


def gather_blocks(gradient, source, used):
    slots = source.shape[0]
    _, rows, columns = gradient.shape
    return pl.pallas_call(
        gather_kernel,
        grid_spec=pltpu.PrefetchScalarGridSpec(
            num_scalar_prefetch=2,
            grid=(slots,),
            in_specs=[pl.BlockSpec((1, rows, columns), lambda s, source, used: (source[s], 0, 0))],
            out_specs=pl.BlockSpec((1, rows, columns), lambda s, source, used: (s, 0, 0)),
        ),
        out_shape=jax.ShapeDtypeStruct((slots, rows, columns), jnp.float32),
    )(source, used, gradient)


def direction_kernel(target_ref, ratio_ref, momentum_ref, returned_ref, out_ref):
    ratio = ratio_ref[pl.program_id(0)]
    out_ref[...] = momentum_decay * momentum_ref[...] + ratio * returned_ref[...]


def directions(momentum, returned, target, ratio):
    blocks, rows, columns = momentum.shape
    return pl.pallas_call(
        direction_kernel,
        grid_spec=pltpu.PrefetchScalarGridSpec(
            num_scalar_prefetch=2,
            grid=(blocks,),
            in_specs=[
                pl.BlockSpec((1, rows, columns), lambda k, target, ratio: (k, 0, 0)),
                pl.BlockSpec((1, rows, columns), lambda k, target, ratio: (target[k], 0, 0)),
            ],
            out_specs=pl.BlockSpec((1, rows, columns), lambda k, target, ratio: (k, 0, 0)),
        ),
        out_shape=jax.ShapeDtypeStruct((blocks, rows, columns), jnp.float32),
    )(target, ratio, momentum, returned)


def halves(value):
    high = value.astype(jnp.bfloat16)
    low = (value - high.astype(jnp.float32)).astype(jnp.bfloat16)
    return high, low


def put_left(ref, rows, value):
    n = ref.shape[1] // 3
    high, low = halves(value)
    ref[rows, 0:n] = high
    ref[rows, n : 2 * n] = high
    ref[rows, 2 * n : 3 * n] = low


def put_right(ref, start, count, value):
    n = ref.shape[0] // 3
    high, low = halves(value)
    ref[pl.ds(start, count), :] = high
    ref[pl.ds(n + start, count), :] = low
    ref[pl.ds(2 * n + start, count), :] = high


def chunks(n, body):
    @pl.loop(0, n // ROWS)
    def _(index):
        start = pl.multiple_of(index * ROWS, ROWS)
        body(start, pl.ds(start, ROWS))


def dot(left, rows, right):
    return jnp.dot(left[rows, :], right[...], preferred_element_type=jnp.float32)


def eye_part(start, n):
    row = lax.broadcasted_iota(jnp.int32, (ROWS, n), 0) + start
    return row == lax.broadcasted_iota(jnp.int32, (ROWS, n), 1)


def new_factor(state, left, right, total, n):
    total[...] = jnp.zeros_like(total)

    def part(start, rows):
        value = factor_decay * state[rows, :] + (1.0 - factor_decay) * dot(left, rows, right)
        state[rows, :] = value
        shifted = value + jnp.where(eye_part(start, n), root_eps, 0.0)
        square = jnp.sum(shifted * shifted, axis=0, keepdims=True)
        total[...] += jnp.broadcast_to(jnp.sum(square, axis=1, keepdims=True), total.shape)

    chunks(n, part)


def inverse_root(state, total, left, right, one, two, emit, n):
    scale = jnp.sqrt(total[0:1, 0:1])
    coefficient = lax.rsqrt(jnp.sqrt(scale))
    inverse = 1.0 / scale

    def first(start, rows):
        value = (state[rows, :] + jnp.where(eye_part(start, n), root_eps, 0.0)) * inverse
        one[rows, :] = value
        put_left(left, rows, value)
        put_right(right, start, ROWS, value)

    chunks(n, first)

    def second(start, rows):
        two[rows, :] = dot(left, rows, right)

    chunks(n, second)

    def split_second(start, rows):
        put_right(right, start, ROWS, two[rows, :])

    chunks(n, split_second)

    def third(start, rows):
        cube = dot(left, rows, right)
        m, m2 = one[rows, :], two[rows, :]
        one[rows, :] = jnp.where(eye_part(start, n), ROOT[0], 0.0) + ROOT[1] * m + ROOT[2] * m2 + ROOT[3] * cube
        two[rows, :] = ROOT[4] * m + ROOT[5] * m2 + ROOT[6] * cube
        put_left(left, rows, cube)

    chunks(n, third)

    def split_third(start, rows):
        put_right(right, start, ROWS, two[rows, :])

    chunks(n, split_third)

    def last(start, rows):
        emit(start, rows, coefficient * (one[rows, :] + dot(left, rows, right)))

    chunks(n, last)


def step_kernel(
    n_dp, n_t, near,
    out_ref, adam_ref, left_hbm, right_hbm,
    ret_ref, adam_all, sum_all, left_out, right_out,
    stage, gbuf, lbuf, rbuf, pbuf, psum, total, one, two,
    g_left, g_right, gt_left, gt_right, w_left, w_right, x_left, x_right,
    s1, r1, s2, r2, s3, r3, s4, r4, s5, r5, lsem, rsem, losem, rosem,
):
    i = lax.axis_index("dp")
    t = lax.axis_index("tensor")
    rows = out_ref.shape[2]
    n = lbuf.shape[1]
    slots = 2 * near

    def load(index):
        return (
            pltpu.make_async_copy(left_hbm.at[index], lbuf.at[index], lsem.at[index]),
            pltpu.make_async_copy(right_hbm.at[index], rbuf.at[index], rsem.at[index]),
        )

    def save(index):
        return (
            pltpu.make_async_copy(lbuf.at[index], left_out.at[index], losem.at[index]),
            pltpu.make_async_copy(rbuf.at[index], right_out.at[index], rosem.at[index]),
        )

    barrier = pltpu.get_barrier_semaphore()
    for a in range(n_dp):
        for b in range(n_t):
            @pl.when(jnp.logical_not((i == a) & (t == b)))
            def _():
                pl.semaphore_signal(barrier, inc=1, device_id=(a, b), device_id_type=MESH)
    pl.semaphore_wait(barrier, n_dp * n_t - 1)

    def spread(r, step):
        other = lax.rem(i + step, n_dp)
        return pltpu.make_async_remote_copy(
            src_ref=out_ref.at[other, r], dst_ref=stage.at[r, i],
            send_sem=s1.at[r, step], recv_sem=r1.at[r, i],
            device_id=(other, t), device_id_type=MESH,
        )

    def forward(r, j):
        return pltpu.make_async_remote_copy(
            src_ref=stage.at[r, j], dst_ref=gbuf.at[r, lax.rem(j, near), t],
            send_sem=s2.at[r, j], recv_sem=r2.at[r, lax.rem(j, near), t],
            device_id=(i, j // near), device_id_type=MESH,
        )

    def forward_here(r, j):
        return pltpu.make_async_copy(
            stage.at[r, j], gbuf.at[r, lax.rem(j, near), t], r2.at[r, lax.rem(j, near), t]
        )

    def own(r):
        return pltpu.make_async_copy(out_ref.at[i, r], stage.at[r, i], r1.at[r, i])

    def adam_copy(step):
        return pltpu.make_async_remote_copy(
            src_ref=adam_ref, dst_ref=adam_all.at[t],
            send_sem=s5.at[step], recv_sem=r5.at[t],
            device_id=(i, lax.rem(t + step, n_t)), device_id_type=MESH,
        )

    adam_here = pltpu.make_async_copy(adam_ref, adam_all.at[t], r5.at[t])

    def home(r, b, q):
        return pltpu.make_async_remote_copy(
            src_ref=pbuf.at[r, b, pl.ds(pl.multiple_of(q * rows, rows), rows)], dst_ref=ret_ref.at[i, r],
            send_sem=s3.at[r, b, q], recv_sem=r3.at[r, i],
            device_id=(t * near + b, q), device_id_type=MESH,
        )

    def home_here(r, b, q):
        return pltpu.make_async_copy(
            pbuf.at[r, b, pl.ds(pl.multiple_of(q * rows, rows), rows)], ret_ref.at[i, r], r3.at[r, i]
        )

    def home_sum(r, b, q):
        return pltpu.make_async_remote_copy(
            src_ref=psum.at[r, b], dst_ref=sum_all.at[i, r],
            send_sem=s4.at[r, b, q], recv_sem=r4.at[r, i],
            device_id=(t * near + b, q), device_id_type=MESH,
        )

    def home_sum_here(r, b, q):
        return pltpu.make_async_copy(psum.at[r, b], sum_all.at[i, r], r4.at[r, i])

    for r in range(2):
        own(r).start()
        for step in range(1, n_dp):
            spread(r, step).start()
    adam_here.start()
    for step in range(1, n_t):
        adam_copy(step).start()
    for index in range(slots):
        for copy in load(index):
            copy.start()

    for r in range(2):
        for step in range(n_dp):
            j = lax.rem(i + n_dp - step, n_dp)
            pltpu.make_async_copy(stage.at[r, j], stage.at[r, j], r1.at[r, j]).wait()
            same = j // near == t

            @pl.when(same)
            def _():
                forward_here(r, j).start()

            @pl.when(jnp.logical_not(same))
            def _():
                forward(r, j).start()

    @pl.loop(0, slots)
    def _(q):
        r = q // near
        b = lax.rem(q, near)
        index = b * 2 + r
        for copy in load(index):
            copy.wait()
        for part in range(n_t):
            pltpu.make_async_copy(gbuf.at[r, b, part], gbuf.at[r, b, part], r2.at[r, b, part]).wait()
        left, right = lbuf.at[index], rbuf.at[index]
        for part in range(n_t):
            here = pl.ds(part * rows, rows)
            value = gbuf[r, b, part]
            put_left(g_left, here, value)
            put_right(g_right, part * rows, rows, value)
            one[here, :] = value

        def turn(start, here):
            value = jnp.transpose(one[:, here])
            put_left(gt_left, here, value)
            put_right(gt_right, start, ROWS, value)

        for start in range(0, n, ROWS):
            turn(start, pl.ds(start, ROWS))
        new_factor(left, g_left, gt_right, total.at[0], n)
        new_factor(right, gt_left, g_right, total.at[1], n)
        for copy in save(index):
            copy.start()

        def keep_left(start, here, value):
            put_left(x_left, here, value)

        def keep_right(start, here, value):
            put_right(x_right, start, ROWS, value)

        inverse_root(left, total.at[0], w_left, w_right, one, two, keep_left, n)
        inverse_root(right, total.at[1], w_left, w_right, one, two, keep_right, n)

        def middle(start, here):
            put_left(w_left, here, dot(x_left, here, g_right))

        chunks(n, middle)
        psum[r, b] = jnp.zeros(psum.shape[2:], jnp.float32)

        def final(start, here):
            value = dot(w_left, here, x_right)
            pbuf[r, b, here, :] = value
            square = jnp.sum(value * value, axis=0, keepdims=True)
            psum[r, b] += jnp.broadcast_to(jnp.sum(square, axis=1, keepdims=True), psum.shape[2:])

        chunks(n, final)
        for part in range(n_t):
            mine = (t * near + b == i) & (t == part)

            @pl.when(mine)
            def _():
                home_here(r, b, part).start()
                home_sum_here(r, b, part).start()

            @pl.when(jnp.logical_not(mine))
            def _():
                home(r, b, part).start()
                home_sum(r, b, part).start()

    for r in range(2):
        for step in range(1, n_dp):
            spread(r, step).wait_send()
        for j in range(n_dp):
            @pl.when(j // near != t)
            def _():
                forward(r, j).wait_send()
    for step in range(1, n_t):
        adam_copy(step).wait_send()
    for index in range(slots):
        for copy in save(index):
            copy.wait()
    for part in range(n_t):
        pltpu.make_async_copy(adam_all.at[part], adam_all.at[part], r5.at[part]).wait()
    for r in range(2):
        for b in range(near):
            for part in range(n_t):
                @pl.when(jnp.logical_not((t * near + b == i) & (t == part)))
                def _():
                    home(r, b, part).wait_send()
                    home_sum(r, b, part).wait_send()
        for o in range(n_dp):
            pltpu.make_async_copy(ret_ref.at[o, r], ret_ref.at[o, r], r3.at[r, o]).wait()
            pltpu.make_async_copy(sum_all.at[o, r], sum_all.at[o, r], r4.at[r, o]).wait()


def step(outgoing, adam, left_old, right_old, n_dp, n_t):
    near = n_dp // n_t
    slots = 2 * near
    _, _, rows, n = outgoing.shape
    f32, bf16 = jnp.float32, jnp.bfloat16
    vmem = pl.BlockSpec(memory_space=pltpu.VMEM)
    hbm = pl.BlockSpec(memory_space=pl.ANY)
    dma = pltpu.SemaphoreType.DMA
    wide, tall = pltpu.VMEM((n, 3 * n), bf16), pltpu.VMEM((3 * n, n), bf16)
    return pl.pallas_call(
        functools.partial(step_kernel, n_dp, n_t, near),
        out_shape=(
            jax.ShapeDtypeStruct((n_dp, 2, rows, n), f32),
            jax.ShapeDtypeStruct((n_t,) + adam.shape, f32),
            jax.ShapeDtypeStruct((n_dp, 2, 8, 128), f32),
            jax.ShapeDtypeStruct((slots, n, n), f32),
            jax.ShapeDtypeStruct((slots, n, n), f32),
        ),
        in_specs=[vmem, vmem, hbm, hbm],
        out_specs=(hbm, vmem, vmem, hbm, hbm),
        scratch_shapes=[
            pltpu.VMEM((2, n_dp, rows, n), f32),
            pltpu.VMEM((2, near, n_t, rows, n), f32),
            pltpu.VMEM((slots, n, n), f32),
            pltpu.VMEM((slots, n, n), f32),
            pltpu.VMEM((2, near, n, n), f32),
            pltpu.VMEM((2, near, 8, 128), f32),
            pltpu.VMEM((2, 8, 128), f32),
            pltpu.VMEM((n, n), f32),
            pltpu.VMEM((n, n), f32),
            wide, tall, wide, tall, wide, tall, wide, tall,
            dma((2, n_dp)), dma((2, n_dp)),
            dma((2, n_dp)), dma((2, near, n_t)),
            dma((2, near, n_t)), dma((2, n_dp)),
            dma((2, near, n_t)), dma((2, n_dp)),
            dma((n_t,)), dma((n_t,)),
            dma((slots,)), dma((slots,)), dma((slots,)), dma((slots,)),
        ],
        compiler_params=pltpu.CompilerParams(
            collective_id=0, has_side_effects=True, vmem_limit_bytes=56 * 2**20
        ),
    )(outgoing, adam, left_old, right_old)


def per_device(gradient, second_moment, momentum, left_state, right_state, owner):
    dp_count = lax.axis_size("dp")
    tensor_count = lax.axis_size("tensor")
    blocks_here, rows, columns = gradient.shape
    slots_dp = PAIR_MOST * dp_count
    owners = owner[:, 0]
    position = jnp.arange(blocks_here, dtype=jnp.int32)
    earlier = (owners[:, None] == owners[None, :]) & (position[None, :] < position[:, None])
    rank = jnp.sum(earlier.astype(jnp.int32), axis=1)
    target = owners * PAIR_MOST + rank
    select = (target[None, :] == jnp.arange(slots_dp, dtype=jnp.int32)[:, None]).astype(jnp.int32)
    source = jnp.sum(select * position[None, :], axis=1)
    used = jnp.sum(select, axis=1)
    outgoing = gather_blocks(gradient, source, used).reshape(dp_count, PAIR_MOST, rows, columns)
    moment_new = adam_decay * second_moment + (1.0 - adam_decay) * gradient * gradient
    adam = gradient / (jnp.sqrt(moment_new) + adam_eps)
    adam_part = jnp.sum(adam * adam, axis=(1, 2))
    padded = -(-blocks_here // 8) * 8
    adam_tile = jnp.broadcast_to(jnp.pad(adam_part, (0, padded - blocks_here))[:, None], (padded, 128))
    returned, adam_all, sums, left_new, right_new = step(
        outgoing, adam_tile, left_state[0], right_state[0], dp_count, tensor_count
    )
    adam_sum = jnp.sum(adam_all[:, :blocks_here, 0], axis=0)
    pre_sum = jnp.sum(
        jnp.where(select.T > 0, sums[:, :, 0, 0].reshape(1, slots_dp), 0.0), axis=1
    )
    area = float(columns * columns)
    ratio = jnp.sqrt(adam_sum / area / (pre_sum / area + mean_eps))
    direction = directions(momentum, returned.reshape(slots_dp, rows, columns), target, ratio)
    return (direction, moment_new, left_new[None], right_new[None])


def solution(mesh):
    return jax.shard_map(
        per_device,
        mesh=mesh,
        in_specs=(
            P("dp", "tensor", None),
            P("dp", "tensor", None),
            P("dp", "tensor", None),
            P("dp", "tensor", None, None),
            P("dp", "tensor", None, None),
            P("dp", None),
        ),
        out_specs=(
            P("dp", "tensor", None),
            P("dp", "tensor", None),
            P("dp", "tensor", None, None),
            P("dp", "tensor", None, None),
        ),
        check_vma=False,
    )
```

time: 487 us -> 246 us (0.51)
  the two profiles are of different devices: /device:TPU:0 before, /device:TPU:25 now
where the time goes in v1:
time: 246 us; the launch traced here: 245 us
  Pallas kernels  226 us (92%)
  other arithmetic  10 us (4%)
  local copies, waits for them, and re-layouts  8.54 us (3%)
    pallas_call x1, Pallas kernels, step(): pl.pallas_call(functools.partial(step_kernel, n_dp, n_t, near), out_shape...  206 us
    pallas_call x1, Pallas kernels, gather_blocks(): pl.pallas_call(gather_kernel, grid_spec=pltpu.PrefetchScalarGridSpec(num_...  10.9 us
    pallas_call x1, Pallas kernels, directions(): pl.pallas_call(direction_kernel, grid_spec=pltpu.PrefetchScalarGridSpec(n...  9.16 us
    unnamed x6, local copies, waits for them, and re-layouts  6.84 us
    reduce_sum x1, other arithmetic, per_device(): adam_part = jnp.sum(adam * adam, axis=(1, 2))  6.13 us

profile of v1, /device:TPU:25, one launch (start us, length us, event | category | flops | bytes accessed | tf_op | source)
XLA Modules:
  0.0 245.3 jit_solution(16103406100390798796)
XLA Ops:
  0.6 0.9 convert_reduce_fusion.1
  1.5 0.7 multiply_add_fusion.target_ref
  2.2 0.0 copy-start.1
  2.2 0.7 convert_reduce_fusion
  2.9 6.1 %multiply_reduce_fusion = (f32[12]{0:T(128)S(1)}, f32[12,128,512]{2,1,0:T(8,128)}) fusion(f32[12,128,512]{2,1,0:T(8,128)} %gradient_ref.1, f32[12,128,512]{2,1,0:T(8,128)} %param.7), kind=kLoop, calls=%fused_computation.2 | loop fusion | flops 6291444 | bytes 9437232 | tf_op jit(solution)/shard_map/reduce_sum | solution.py:433
  9.1 0.7 broadcast_in_dim.31.adam_ref
  9.7 10.9 %shard_map.93 = f32[16,128,512]{2,1,0:T(8,128)} custom-call(s32[16]{0:T(128)} %get-tuple-element.15.source_ref, s32[16]{0:T(128)} %get-tuple-element.14.used_ref, f32[12,128,512]{2,1,0:T(8,128)} %gradient_ref.1), custom_call_target="tpu_custom_call" | custom-call | tf_op jit(solution)/shard_map/pallas_call | solution.py:42
  20.6 206.1 %shard_map.94 = (f32[8,2,128,512]{3,2,1,0:T(8,128)}, f32[4,16,128]{2,1,0:T(8,128)}, f32[8,2,8,128]{3,2,1,0:T(8,128)}, f32[4,512,512]{2,1,0:T(8,128)}, f32[4,512,512]{2,1,0:T(8,128)}) custom-call(f32[8,2,128,512]{3,2,1,0:T(8,128)} %bitcast.8, f32[16,128]{1,0:T(8,128)} %broadcast_in_dim.31.adam_ref, f32[4,512,512]{2,1,0:T(8,128)} %bitcast.12, ...), custom_call_target="tpu_custom_call" | custom-call | tf_op jit(solution)/shard_map/pallas_call | solution.py:382
  226.7 0.9 slice_reduce_fusion
  227.6 0.9 slice_reduce_fusion.1
  228.5 0.1 broadcast_in_dim.32
  228.6 0.0 copy-done.1
  228.6 0.2 select_reduce_fusion
  228.8 0.5 fusion.2.ratio_ref
  229.3 9.2 %shard_map.95 = f32[12,128,512]{2,1,0:T(8,128)} custom-call(s32[12]{0:T(128)} %copy-done.1, f32[12]{0:T(128)} %fusion.2.ratio_ref, f32[12,128,512]{2,1,0:T(8,128)} %momentum_ref.1, f32[16,128,512]{2,1,0:T(8,128)} %bitcast.11), custom_call_target="tpu_custom_call" | custom-call | tf_op jit(solution)/shard_map/pallas_call | solution.py:61
  238.5 0.0 copy-start
  238.5 4.8 %copy.12 = f32[1,4,512,512]{3,2,1,0:T(8,128)} copy(f32[1,4,512,512]{3,2,1,0:T(8,128)} %bitcast.10) | data formatting | bytes 8388608
  243.3 0.0 copy-done
  243.3 2.0 copy.13
  (1 shorter events, 0.0 us)
Async XLA Ops:
  2.2 226.4 %copy-start.1 = (s32[12]{0:T(128)}, s32[12]{0:T(128)S(1)}, u32[]{:S(2)}) copy-start(s32[12]{0:T(128)S(1)} %multiply_add_fusion.target_ref) | copy-start | bytes 148
  238.5 4.8 %copy-start = (f32[4,512,512]{2,1,0:T(8,128)S(1)}, f32[4,512,512]{2,1,0:T(8,128)}, u32[]{:S(2)}) copy-start(f32[4,512,512]{2,1,0:T(8,128)} %get-tuple-element.13) | copy-start | bytes 12582916

commit v2 on v1

--- a/solution.py
+++ b/solution.py
@@ -31,46 +31,38 @@
 )
 
 
-def gather_kernel(source_ref, used_ref, gradient_ref, out_ref):
-    used = used_ref[pl.program_id(0)] > 0
-    out_ref[...] = jnp.where(used, gradient_ref[...], 0.0)
+def gather_kernel(source_ref, used_ref, gradient_ref, out_ref, sems):
+    slots = out_ref.shape[0]
+    for s in range(slots):
+        used = used_ref[s] > 0
+
+        @pl.when(used)
+        def _():
+            pltpu.make_async_copy(gradient_ref.at[source_ref[s]], out_ref.at[s], sems.at[s]).start()
+
+        @pl.when(jnp.logical_not(used))
+        def _():
+            out_ref[s] = jnp.zeros(out_ref.shape[1:], jnp.float32)
+
+    for s in range(slots):
+        @pl.when(used_ref[s] > 0)
+        def _():
+            pltpu.make_async_copy(gradient_ref.at[0], out_ref.at[s], sems.at[s]).wait()
 
 
 def gather_blocks(gradient, source, used):
     slots = source.shape[0]
     _, rows, columns = gradient.shape
+    smem = pl.BlockSpec(memory_space=pltpu.SMEM)
+    hbm = pl.BlockSpec(memory_space=pl.ANY)
     return pl.pallas_call(
         gather_kernel,
-        grid_spec=pltpu.PrefetchScalarGridSpec(
-            num_scalar_prefetch=2,
-            grid=(slots,),
-            in_specs=[pl.BlockSpec((1, rows, columns), lambda s, source, used: (source[s], 0, 0))],
-            out_specs=pl.BlockSpec((1, rows, columns), lambda s, source, used: (s, 0, 0)),
-        ),
+        in_specs=[smem, smem, hbm],
+        out_specs=pl.BlockSpec(memory_space=pltpu.VMEM),
         out_shape=jax.ShapeDtypeStruct((slots, rows, columns), jnp.float32),
+        scratch_shapes=[pltpu.SemaphoreType.DMA((slots,))],
+        compiler_params=pltpu.CompilerParams(vmem_limit_bytes=56 * 2**20),
     )(source, used, gradient)
-
-
-def direction_kernel(target_ref, ratio_ref, momentum_ref, returned_ref, out_ref):
-    ratio = ratio_ref[pl.program_id(0)]
-    out_ref[...] = momentum_decay * momentum_ref[...] + ratio * returned_ref[...]
-
-
-def directions(momentum, returned, target, ratio):
-    blocks, rows, columns = momentum.shape
-    return pl.pallas_call(
-        direction_kernel,
-        grid_spec=pltpu.PrefetchScalarGridSpec(
-            num_scalar_prefetch=2,
-            grid=(blocks,),
-            in_specs=[
-                pl.BlockSpec((1, rows, columns), lambda k, target, ratio: (k, 0, 0)),
-                pl.BlockSpec((1, rows, columns), lambda k, target, ratio: (target[k], 0, 0)),
-            ],
-            out_specs=pl.BlockSpec((1, rows, columns), lambda k, target, ratio: (k, 0, 0)),
-        ),
-        out_shape=jax.ShapeDtypeStruct((blocks, rows, columns), jnp.float32),
-    )(target, ratio, momentum, returned)
 
 
 def halves(value):
@@ -169,11 +161,12 @@
 
 def step_kernel(
     n_dp, n_t, near,
-    out_ref, adam_ref, left_hbm, right_hbm,
-    ret_ref, adam_all, sum_all, left_out, right_out,
+    target_ref, out_ref, gradient_hbm, second_hbm, momentum_hbm, left_hbm, right_hbm,
+    direction_out, moment_out, left_out, right_out,
+    gradient, second, momentum, ret_ref, adam_ref, adam_all, sum_all,
     stage, gbuf, lbuf, rbuf, pbuf, psum, total, one, two,
     g_left, g_right, gt_left, gt_right, w_left, w_right, x_left, x_right,
-    s1, r1, s2, r2, s3, r3, s4, r4, s5, r5, lsem, rsem, losem, rosem,
+    s1, r1, s2, r2, s3, r3, s4, r4, s5, r5, lsem, rsem, losem, rosem, fsem, dsem, msem,
 ):
     i = lax.axis_index("dp")
     t = lax.axis_index("tensor")
@@ -259,14 +252,43 @@
         own(r).start()
         for step in range(1, n_dp):
             spread(r, step).start()
-    adam_here.start()
-    for step in range(1, n_t):
-        adam_copy(step).start()
+    fetch = [
+        pltpu.make_async_copy(gradient_hbm, gradient, fsem.at[0]),
+        pltpu.make_async_copy(second_hbm, second, fsem.at[1]),
+        pltpu.make_async_copy(momentum_hbm, momentum, fsem.at[2]),
+    ]
+    for copy in fetch:
+        copy.start()
     for index in range(slots):
         for copy in load(index):
             copy.start()
 
+    blocks = gradient.shape[0]
+
+    def block_moment(k):
+        return pltpu.make_async_copy(second.at[k], moment_out.at[k], msem.at[k])
+
+    def block_direction(k):
+        return pltpu.make_async_copy(momentum.at[k], direction_out.at[k], dsem.at[k])
+
     for r in range(2):
+        if r == 1:
+            fetch[0].wait()
+            fetch[1].wait()
+
+            @pl.loop(0, blocks)
+            def _(k):
+                value = gradient[k]
+                moment = adam_decay * second[k] + (1.0 - adam_decay) * value * value
+                second[k] = moment
+                adam = value / (jnp.sqrt(moment) + adam_eps)
+                square = jnp.sum(adam * adam, axis=0, keepdims=True)
+                adam_ref[k] = jnp.broadcast_to(jnp.sum(square, axis=1, keepdims=True), adam_ref.shape[1:])
+                block_moment(k).start()
+
+            adam_here.start()
+            for step in range(1, n_t):
+                adam_copy(step).start()
         for step in range(n_dp):
             j = lax.rem(i + n_dp - step, n_dp)
             pltpu.make_async_copy(stage.at[r, j], stage.at[r, j], r1.at[r, j]).wait()
@@ -344,6 +366,7 @@
                 home(r, b, part).start()
                 home_sum(r, b, part).start()
 
+    fetch[2].wait()
     for r in range(2):
         for step in range(1, n_dp):
             spread(r, step).wait_send()
@@ -369,28 +392,52 @@
             pltpu.make_async_copy(ret_ref.at[o, r], ret_ref.at[o, r], r3.at[r, o]).wait()
             pltpu.make_async_copy(sum_all.at[o, r], sum_all.at[o, r], r4.at[r, o]).wait()
 
-
-def step(outgoing, adam, left_old, right_old, n_dp, n_t):
+    area = float(n * n)
+
+    @pl.loop(0, blocks)
+    def _(k):
+        target = target_ref[k]
+        other, r = target // 2, lax.rem(target, 2)
+        adam_sum = adam_all[0, k]
+        for part in range(1, n_t):
+            adam_sum = adam_sum + adam_all[part, k]
+        ratio = jnp.sqrt(adam_sum / area / (sum_all[other, r] / area + mean_eps))
+        momentum[k] = momentum_decay * momentum[k] + ratio[0:1, 0:1] * ret_ref[other, r]
+        block_direction(k).start()
+
+    @pl.loop(0, blocks)
+    def _(k):
+        block_moment(k).wait()
+        block_direction(k).wait()
+
+
+def step(target, outgoing, gradient, second, momentum, left_old, right_old, n_dp, n_t):
     near = n_dp // n_t
     slots = 2 * near
     _, _, rows, n = outgoing.shape
+    blocks = gradient.shape[0]
     f32, bf16 = jnp.float32, jnp.bfloat16
-    vmem = pl.BlockSpec(memory_space=pltpu.VMEM)
     hbm = pl.BlockSpec(memory_space=pl.ANY)
     dma = pltpu.SemaphoreType.DMA
     wide, tall = pltpu.VMEM((n, 3 * n), bf16), pltpu.VMEM((3 * n, n), bf16)
     return pl.pallas_call(
         functools.partial(step_kernel, n_dp, n_t, near),
         out_shape=(
-            jax.ShapeDtypeStruct((n_dp, 2, rows, n), f32),
-            jax.ShapeDtypeStruct((n_t,) + adam.shape, f32),
-            jax.ShapeDtypeStruct((n_dp, 2, 8, 128), f32),
+            jax.ShapeDtypeStruct(gradient.shape, f32),
+            jax.ShapeDtypeStruct(gradient.shape, f32),
             jax.ShapeDtypeStruct((slots, n, n), f32),
             jax.ShapeDtypeStruct((slots, n, n), f32),
         ),
-        in_specs=[vmem, vmem, hbm, hbm],
-        out_specs=(hbm, vmem, vmem, hbm, hbm),
+        in_specs=[pl.BlockSpec(memory_space=pltpu.SMEM)] + [hbm] * 6,
+        out_specs=(hbm, hbm, hbm, hbm),
         scratch_shapes=[
+            pltpu.VMEM(gradient.shape, f32),
+            pltpu.VMEM(gradient.shape, f32),
+            pltpu.VMEM(gradient.shape, f32),
+            pltpu.VMEM((n_dp, 2, rows, n), f32),
+            pltpu.VMEM((blocks, 8, 128), f32),
+            pltpu.VMEM((n_t, blocks, 8, 128), f32),
+            pltpu.VMEM((n_dp, 2, 8, 128), f32),
             pltpu.VMEM((2, n_dp, rows, n), f32),
             pltpu.VMEM((2, near, n_t, rows, n), f32),
             pltpu.VMEM((slots, n, n), f32),
@@ -407,11 +454,12 @@
             dma((2, near, n_t)), dma((2, n_dp)),
             dma((n_t,)), dma((n_t,)),
             dma((slots,)), dma((slots,)), dma((slots,)), dma((slots,)),
+            dma((3,)), dma((blocks,)), dma((blocks,)),
         ],
         compiler_params=pltpu.CompilerParams(
             collective_id=0, has_side_effects=True, vmem_limit_bytes=56 * 2**20
         ),
-    )(outgoing, adam, left_old, right_old)
+    )(target, outgoing, gradient, second, momentum, left_old, right_old)
 
 
 def per_device(gradient, second_moment, momentum, left_state, right_state, owner):
@@ -428,21 +476,10 @@
     source = jnp.sum(select * position[None, :], axis=1)
     used = jnp.sum(select, axis=1)
     outgoing = gather_blocks(gradient, source, used).reshape(dp_count, PAIR_MOST, rows, columns)
-    moment_new = adam_decay * second_moment + (1.0 - adam_decay) * gradient * gradient
-    adam = gradient / (jnp.sqrt(moment_new) + adam_eps)
-    adam_part = jnp.sum(adam * adam, axis=(1, 2))
-    padded = -(-blocks_here // 8) * 8
-    adam_tile = jnp.broadcast_to(jnp.pad(adam_part, (0, padded - blocks_here))[:, None], (padded, 128))
-    returned, adam_all, sums, left_new, right_new = step(
-        outgoing, adam_tile, left_state[0], right_state[0], dp_count, tensor_count
+    direction, moment_new, left_new, right_new = step(
+        target, outgoing, gradient, second_moment, momentum, left_state[0], right_state[0],
+        dp_count, tensor_count,
     )
-    adam_sum = jnp.sum(adam_all[:, :blocks_here, 0], axis=0)
-    pre_sum = jnp.sum(
-        jnp.where(select.T > 0, sums[:, :, 0, 0].reshape(1, slots_dp), 0.0), axis=1
-    )
-    area = float(columns * columns)
-    ratio = jnp.sqrt(adam_sum / area / (pre_sum / area + mean_eps))
-    direction = directions(momentum, returned.reshape(slots_dp, rows, columns), target, ratio)
     return (direction, moment_new, left_new[None], right_new[None])
 
 

time: 246 us -> 238 us (0.967)
  other arithmetic: 10 us -> 2.2 us
  Pallas kernels: 226 us -> 221 us
  local copies, waits for them, and re-layouts: 8.54 us -> 13.1 us
    pallas_call x2 -> x1, Pallas kernels: 20.1 us -> 4.68 us  [gather_blocks(): pl.pallas_call(gather_kernel, in_specs=[smem, smem, hbm], out_specs=pl.Bl...]
    pallas_call x1, Pallas kernels: 206 us -> 217 us  [step(): pl.pallas_call(functools.partial(step_kernel, n_dp, n_t, near), out_shape...]
    reduce_sum x3 -> x0, other arithmetic: 7.19 us -> none  [the longest x1 6.13 us: per_device(): adam_part = jnp.sum(adam * adam, axis=(1, 2))]
    unnamed x6 -> x12, local copies, waits for them, and re-layouts: 6.84 us -> 13.1 us
where the time goes in v2:
time: 238 us; the launch traced here: 237 us
  Pallas kernels  221 us (93%)
  local copies, waits for them, and re-layouts  13.1 us (6%)
    pallas_call x1, Pallas kernels, step(): pl.pallas_call(functools.partial(step_kernel, n_dp, n_t, near), out_shape...  217 us
    unnamed x12, local copies, waits for them, and re-layouts  13.1 us

profile of v2, /device:TPU:25, one launch (start us, length us, event | category | flops | bytes accessed | tf_op | source)
XLA Modules:
  0.0 237.3 jit_solution(3870705240604241502)
XLA Ops:
  0.6 0.9 convert_reduce_fusion.1
  1.5 0.7 multiply_add_fusion.target_ref
  2.2 0.0 copy-start.3
  2.2 0.6 convert_reduce_fusion
  2.8 4.7 %shard_map.93 = f32[16,128,512]{2,1,0:T(8,128)} custom-call(s32[16]{0:T(128)} %get-tuple-element.13.source_ref, s32[16]{0:T(128)} %get-tuple-element.12.used_ref, f32[12,128,512]{2,1,0:T(8,128)} %gradient_hbm.1), custom_call_target="tpu_custom_call" | custom-call | tf_op jit(solution)/shard_map/pallas_call | solution.py:58
  7.5 0.0 copy-done.3
  7.5 216.7 %shard_map.94 = (f32[12,128,512]{2,1,0:T(8,128)}, f32[12,128,512]{2,1,0:T(8,128)}, f32[4,512,512]{2,1,0:T(8,128)}, f32[4,512,512]{2,1,0:T(8,128)}) custom-call(s32[12]{0:T(128)} %copy-done.3, f32[8,2,128,512]{3,2,1,0:T(8,128)} %bitcast.7, f32[12,128,512]{2,1,0:T(8,128)} %gradient_hbm.1, f32[12,128,512]{2,1,0:T(8,128)} %second_hbm.1, ...), custom_call_target="tpu_custom_call" | custom-call | tf_op jit(solution)/shard_map/pallas_call | solution.py:423
  224.2 0.0 copy-start.2
  224.2 4.0 %copy.14 = f32[12,128,512]{2,1,0:T(8,128)} copy(f32[12,128,512]{2,1,0:T(8,128)} %get-tuple-element.18) | data formatting | bytes 6291456
  228.3 0.0 copy-done.2
  228.3 0.0 copy-start.1
  228.3 1.7 copy.15
  229.9 1.7 copy-done.1
  231.6 0.0 copy-start
  231.6 2.1 copy.16
  233.7 1.6 copy-done
  235.3 2.0 copy.17
Async XLA Ops:
  2.2 5.3 %copy-start.3 = (s32[12]{0:T(128)}, s32[12]{0:T(128)S(1)}, u32[]{:S(2)}) copy-start(s32[12]{0:T(128)S(1)} %multiply_add_fusion.target_ref) | copy-start | bytes 148
  224.2 4.0 %copy-start.2 = (f32[12,128,512]{2,1,0:T(8,128)S(1)}, f32[12,128,512]{2,1,0:T(8,128)}, u32[]{:S(2)}) copy-start(f32[12,128,512]{2,1,0:T(8,128)} %get-tuple-element.19) | copy-start | bytes 9437188
  228.3 3.3 %copy-start.1 = (f32[4,512,512]{2,1,0:T(8,128)S(1)}, f32[4,512,512]{2,1,0:T(8,128)}, u32[]{:S(2)}) copy-start(f32[4,512,512]{2,1,0:T(8,128)} %get-tuple-element.10) | copy-start | bytes 12582916
  231.6 3.7 %copy-start = (f32[4,512,512]{2,1,0:T(8,128)S(1)}, f32[4,512,512]{2,1,0:T(8,128)}, u32[]{:S(2)}) copy-start(f32[4,512,512]{2,1,0:T(8,128)} %get-tuple-element.11) | copy-start | bytes 12582916
